TPU v7x, 32 devices: a whole 2x2x4 slice. The times are simulated.
32 devices in a mesh: farm: 2 (over x), body: 16 (over z, y, core).
Axes of the slice: x: 2, y: 2, z: 4, core: 2. Of those that a mesh axis runs over, the one named last changes fastest.
Arguments:
- incident: float32 [32, 2, 16, 768], P(('farm', 'body')), parts along dimension 0, may hold values from -6 to 6
- self_inverse: float32 [32, 2, 768, 768], P(('farm', 'body')), parts along dimension 0
- cross_blocks: float32 [32, 4, 2, 768, 768], P(('farm', 'body')), parts along dimension 0, may hold values from -0.046875 to 0.046875
- neighbours: int32 [32, 4], P(('farm', 'body')), parts along dimension 0, may hold values from -1 to 15, as said below
- panel_weight: float32 [32, 768], P(('farm', 'body')), parts along dimension 0, may hold values from -0.0546875 to 0.0546875
Outputs:
- sources: float32 [32, 2, 16, 768], P(('farm', 'body')), parts along dimension 0
- farm_force: float32 [2, 2, 16], P('farm'), parts along dimension 0
There are 2 independent parts, one for each index of `farm`. A program takes and returns all parts, laid end to end along the dimension named above; each array names one. Nothing has to cross between parts.
Inputs may be any that keep to these rules, and one draw needn't show every extreme that they name: `neighbours`: each row names distinct bodies other than its own, each within 8 positions of it around the closed loop of 16 bodies; some body names the body exactly 8 positions away.
All inputs are finite; a program needn't handle non-finite values.
Results may differ from a plain program's by a relative error of at most 0.0003.
Values sent between devices are 32-bit elements; how exact they have to be, the bound alone decides.
A program may use at most 128 MiB of HBM per device.

v0:
```python
import jax
import jax.numpy as jnp
from jax import lax
from jax.sharding import PartitionSpec as P

ITERS = 6


def complex_apply(matrix, field):
    heads = field.shape[1]
    stacked = field.reshape(2 * heads, field.shape[2])
    dims = (((1,), (1,)), ((), ()))
    real_part = lax.dot_general(stacked, matrix[0], dims, precision=lax.Precision.HIGHEST)
    imag_part = lax.dot_general(stacked, matrix[1], dims, precision=lax.Precision.HIGHEST)
    return jnp.stack([real_part[:heads] - imag_part[heads:], real_part[heads:] + imag_part[:heads]])


def body(incident, self_inverse, cross_blocks, neighbours, panel_weight):
    field = incident[0]
    inverse_one = self_inverse[0]
    blocks = cross_blocks[0]
    index_row = neighbours[0]
    flag_row = index_row >= 0
    safe_row = jnp.where(flag_row, index_row, 0)
    slot_count = index_row.shape[0]
    sources = complex_apply(inverse_one, field)
    for sweep in range(ITERS):
        gathered = lax.all_gather(sources[None], "body", axis=0, tiled=True)
        nearby = jnp.take(gathered, safe_row, axis=0)
        total = field
        for slot in range(slot_count):
            total = total - jnp.where(
                flag_row[slot], complex_apply(blocks[slot], nearby[slot]), 0.0
            )
        sources = complex_apply(inverse_one, total)
    partial_force = jnp.einsum(
        "p,chp->ch", panel_weight[0], sources, precision=lax.Precision.HIGHEST
    )
    farm_force = lax.psum(partial_force, "body")
    return (sources[None], farm_force[None])


def solution(mesh):
    return jax.shard_map(
        body,
        mesh=mesh,
        in_specs=(
            P(("farm", "body"), None, None, None),
            P(("farm", "body"), None, None, None),
            P(("farm", "body"), None, None, None, None),
            P(("farm", "body"), None),
            P(("farm", "body"), None),
        ),
        out_specs=(P(("farm", "body"), None, None, None), P("farm", None, None)),
        check_vma=False,
    )
```

profile of v0, /device:TPU:0, one launch (start us, length us, event | category | flops | bytes accessed | tf_op | source)
XLA Modules:
  0.0 540.5 jit_solution(6577915295749978652)
XLA Ops:
  7.2 3.9 fusion.108
  16.7 41.6 %all-gather.13.cloned.1.call-done = f32[32,16,768]{2,1,0:T(8,128)} async-done(((f32[2,16,768]{2,1,0:T(8,128)}), f32[32,16,768]{2,1,0:T(8,128)}) %all-gather.13.cloned.1.call-update) | async-done | bytes 1572880 | tf_op jit(solution)/shard_map/all_gather | solution.py:28
  72.1 4.0 fusion.22
  80.0 3.9 fusion.70
  87.8 4.3 fusion.94
  99.9 38.7 %all-gather.15.cloned.1.call-done = f32[32,16,768]{2,1,0:T(8,128)} async-done(((f32[2,16,768]{2,1,0:T(8,128)}), f32[32,16,768]{2,1,0:T(8,128)}) %all-gather.15.cloned.1.call-update) | async-done | bytes 1572880 | tf_op jit(solution)/shard_map/all_gather | solution.py:28
  152.4 4.0 fusion.20
  160.3 3.9 fusion.68
  168.1 4.0 fusion.92
  180.0 38.7 %all-gather.17.cloned.1.call-done = f32[32,16,768]{2,1,0:T(8,128)} async-done(((f32[2,16,768]{2,1,0:T(8,128)}), f32[32,16,768]{2,1,0:T(8,128)}) %all-gather.17.cloned.1.call-update) | async-done | bytes 1572880 | tf_op jit(solution)/shard_map/all_gather | solution.py:28
  232.5 4.0 fusion.18
  240.4 3.9 fusion.66
  248.2 4.3 fusion.90
  260.4 38.7 %all-gather.19.cloned.1.call-done = f32[32,16,768]{2,1,0:T(8,128)} async-done(((f32[2,16,768]{2,1,0:T(8,128)}), f32[32,16,768]{2,1,0:T(8,128)}) %all-gather.19.cloned.1.call-update) | async-done | bytes 1572880 | tf_op jit(solution)/shard_map/all_gather | solution.py:28
  312.8 4.0 fusion.16
  328.5 4.0 fusion.88
  340.5 38.7 %all-gather.21.cloned.1.call-done = f32[32,16,768]{2,1,0:T(8,128)} async-done(((f32[2,16,768]{2,1,0:T(8,128)}), f32[32,16,768]{2,1,0:T(8,128)}) %all-gather.21.cloned.1.call-update) | async-done | bytes 1572880 | tf_op jit(solution)/shard_map/all_gather | solution.py:28
  392.9 4.0 fusion.14
  400.8 3.9 fusion.62
  408.7 4.3 fusion.86
  420.8 38.7 %all-gather.23.cloned.1.call-done = f32[32,16,768]{2,1,0:T(8,128)} async-done(((f32[2,16,768]{2,1,0:T(8,128)}), f32[32,16,768]{2,1,0:T(8,128)}) %all-gather.23.cloned.1.call-update) | async-done | bytes 1572880 | tf_op jit(solution)/shard_map/all_gather | solution.py:28
  473.3 4.0 fusion.12
  477.3 4.0 fusion.48
  501.3 32.1 %psum.7 = f32[1,2,16]{2,1,0:T(2,128)} all-reduce(f32[1,2,16]{2,1,0:T(2,128)S(1)} %bitcast.457), channel_id=1, replica_groups=mesh['farm'=2,'body'=16] {'body'}, use_global_device_ids=true, to_apply=%region_0.2 | all-reduce | flops 32 | bytes 256 | tf_op jit(solution)/shard_map/psum | solution.py:39
  (157 shorter events, 189.2 us)
Async XLA Ops:
  7.2 493.7 %copy-start = (f32[1,768]{1,0:T(1,128)S(1)}, f32[1,768]{1,0:T(1,128)}, u32[]{:S(2)}) copy-start(f32[1,768]{1,0:T(1,128)} %param.11) | copy-start | bytes 9220
  7.2 4.0 copy-start.1
  7.2 51.1 %all-gather.13.cloned.1.call-start = ((), (), s32[]{:S(2)}) async-start(), calls=%async_computation | async-start | bytes 1671168 | tf_op jit(solution)/shard_map/all_gather | solution.py:28
  7.2 8.8 %copy-start.2 = (s32[1,4]{1,0:T(1,128)S(1)}, s32[1,4]{1,0:T(1,128)}, u32[]{:S(2)}) copy-start(s32[1,4]{1,0:T(1,128)} %param.10) | copy-start | bytes 52
  15.8 122.8 %all-gather.15.cloned.1.call-start = ((), (), s32[]{:S(2)}) async-start(), calls=%async_computation.1 | async-start | bytes 1671168 | tf_op jit(solution)/shard_map/all_gather | solution.py:28
  72.0 22.6 %slice-start = ((s8[4718592]{0:T(1024)(128)(4,1)}), s8[4194304]{0:T(1024)(128)(4,1)S(1)}, s32[]{:S(2)}) async-start(s8[4718592]{0:T(1024)(128)(4,1)} %bitcast.377), calls=%async_computation.6 | async-start | bytes 8388608
  80.0 14.7 %slice-start.1 = ((s8[4718592]{0:T(1024)(128)(4,1)}), s8[524288]{0:T(1024)(128)(4,1)S(1)}, s32[]{:S(2)}) async-start(s8[4718592]{0:T(1024)(128)(4,1)} %bitcast.377), calls=%async_computation.7 | async-start | bytes 1048576
  99.9 118.8 %all-gather.17.cloned.1.call-start = ((), (), s32[]{:S(2)}) async-start(), calls=%async_computation.2 | async-start | bytes 1671168 | tf_op jit(solution)/shard_map/all_gather | solution.py:28
  152.4 22.4 %slice-start.2 = ((s8[4718592]{0:T(1024)(128)(4,1)}), s8[4194304]{0:T(1024)(128)(4,1)S(1)}, s32[]{:S(2)}) async-start(s8[4718592]{0:T(1024)(128)(4,1)} %bitcast.379), calls=%async_computation.8 | async-start | bytes 8388608
  160.3 14.5 %slice-start.3 = ((s8[4718592]{0:T(1024)(128)(4,1)}), s8[524288]{0:T(1024)(128)(4,1)S(1)}, s32[]{:S(2)}) async-start(s8[4718592]{0:T(1024)(128)(4,1)} %bitcast.379), calls=%async_computation.9 | async-start | bytes 1048576
  180.0 119.1 %all-gather.19.cloned.1.call-start = ((), (), s32[]{:S(2)}) async-start(), calls=%async_computation.3 | async-start | bytes 1671168 | tf_op jit(solution)/shard_map/all_gather | solution.py:28
  232.5 22.6 %slice-start.4 = ((s8[4718592]{0:T(1024)(128)(4,1)}), s8[4194304]{0:T(1024)(128)(4,1)S(1)}, s32[]{:S(2)}) async-start(s8[4718592]{0:T(1024)(128)(4,1)} %bitcast.381), calls=%async_computation.10 | async-start | bytes 8388608
  240.4 14.7 %slice-start.5 = ((s8[4718592]{0:T(1024)(128)(4,1)}), s8[524288]{0:T(1024)(128)(4,1)S(1)}, s32[]{:S(2)}) async-start(s8[4718592]{0:T(1024)(128)(4,1)} %bitcast.381), calls=%async_computation.11 | async-start | bytes 1048576
  260.3 118.8 %all-gather.21.cloned.1.call-start = ((), (), s32[]{:S(2)}) async-start(), calls=%async_computation.4 | async-start | bytes 1671168 | tf_op jit(solution)/shard_map/all_gather | solution.py:28
  312.8 22.4 %slice-start.6 = ((s8[4718592]{0:T(1024)(128)(4,1)}), s8[4194304]{0:T(1024)(128)(4,1)S(1)}, s32[]{:S(2)}) async-start(s8[4718592]{0:T(1024)(128)(4,1)} %bitcast.383), calls=%async_computation.12 | async-start | bytes 8388608
  320.7 14.5 %slice-start.7 = ((s8[4718592]{0:T(1024)(128)(4,1)}), s8[524288]{0:T(1024)(128)(4,1)S(1)}, s32[]{:S(2)}) async-start(s8[4718592]{0:T(1024)(128)(4,1)} %bitcast.383), calls=%async_computation.13 | async-start | bytes 1048576
  340.4 119.1 %all-gather.23.cloned.1.call-start = ((), (), s32[]{:S(2)}) async-start(), calls=%async_computation.5 | async-start | bytes 1671168 | tf_op jit(solution)/shard_map/all_gather | solution.py:28
  392.9 22.6 %slice-start.8 = ((s8[4718592]{0:T(1024)(128)(4,1)}), s8[4194304]{0:T(1024)(128)(4,1)S(1)}, s32[]{:S(2)}) async-start(s8[4718592]{0:T(1024)(128)(4,1)} %bitcast.385), calls=%async_computation.14 | async-start | bytes 8388608
  400.8 14.7 %slice-start.9 = ((s8[4718592]{0:T(1024)(128)(4,1)}), s8[524288]{0:T(1024)(128)(4,1)S(1)}, s32[]{:S(2)}) async-start(s8[4718592]{0:T(1024)(128)(4,1)} %bitcast.385), calls=%async_computation.15 | async-start | bytes 1048576
  473.2 22.4 %slice-start.10 = ((s8[4718592]{0:T(1024)(128)(4,1)}), s8[4194304]{0:T(1024)(128)(4,1)S(1)}, s32[]{:S(2)}) async-start(s8[4718592]{0:T(1024)(128)(4,1)} %bitcast.387), calls=%async_computation.16 | async-start | bytes 8388608
  481.3 14.3 %slice-start.11 = ((s8[4718592]{0:T(1024)(128)(4,1)}), s8[524288]{0:T(1024)(128)(4,1)S(1)}, s32[]{:S(2)}) async-start(s8[4718592]{0:T(1024)(128)(4,1)} %bitcast.387), calls=%async_computation.17 | async-start | bytes 1048576
Sparse Core Ops, SparseCore 0:
  15.9 42.3 all-gather.12
  100.0 38.5 all-gather.14
  180.1 38.5 all-gather.16
  260.4 38.5 all-gather.18
  340.6 38.5 all-gather.20
  420.9 38.5 all-gather.22
where the time goes:
time: 551 us; the launch traced here: 540 us
  waiting for transfers between devices  235 us (43%)
  matrix products  224 us (41%)
  blocking collectives  32.1 us (6%)
  other arithmetic  20.8 us (4%)
  between operations  15.4 us (3%)
  local copies, waits for them, and re-layouts  12.8 us (2%)
    all_gather x6, waiting for transfers between devices, body(): gathered = lax.all_gather(sources[None], 'body', axis=0, tiled=True)  235 us
    dot_general x31, matrix products, complex_apply(): lax.dot_general(stacked, matrix[0], dims, precision=lax.Precision.HIGHEST)  113 us
    dot_general x31, matrix products, complex_apply(): lax.dot_general(stacked, matrix[1], dims, precision=lax.Precision.HIGHEST)  110 us
    psum x1, blocking collectives, body(): farm_force = lax.psum(partial_force, 'body')  32.1 us
    sub x6, other arithmetic, body(): total - jnp.where(flag_row[slot], complex_apply(blocks[slot], nearby[slot...  15.2 us
    gather x6, local copies, waits for them, and re-layouts, body(): nearby = jnp.take(gathered, safe_row, axis=0)  11.9 us
  transfers between devices with their start and end apart: 6, of which 6 were waited for; matrix products, arithmetic and copies ran while one was open for 0% of the time, Pallas kernels for 0%

commit v1 on v0

v1 whole, which is shorter than its diff:
```python
import functools

import jax
import jax.numpy as jnp
from jax import lax
from jax.experimental import pallas as pl
from jax.experimental.pallas import tpu as pltpu
from jax.sharding import PartitionSpec as P

ITERS = 6
F32 = jnp.float32
BF16 = jnp.bfloat16


def flip(index, bits):
    bit = 1
    while bit <= bits:
        if bits & bit:
            index = index + bit - 2 * bit * ((index // bit) % 2)
        bit *= 2
    return index


def halves(value):
    high = value.astype(BF16)
    return high, (value - high.astype(F32)).astype(BF16)


def dot_t(left, right):
    return lax.dot_general(left, right, (((1,), (1,)), ((), ())), preferred_element_type=F32)


def put_field(lhs, column, value, heads):
    rows, panels = value.shape
    high, low = halves(value)
    high_t = jnp.concatenate([-high[heads:], high[:heads]], axis=0)
    low_t = jnp.concatenate([-low[heads:], low[:heads]], axis=0)
    lhs[0:rows, column : column + panels] = high
    lhs[rows : 2 * rows, column : column + panels] = low
    lhs[0:rows, column + panels : column + 2 * panels] = high_t
    lhs[rows : 2 * rows, column + panels : column + 2 * panels] = low_t


def multiply(lhs, depth, high, low, out, rows):
    panels = out.shape[1]
    tile = 256
    for start in range(0, panels, tile):
        both = dot_t(lhs[:, 0:depth], high[start : start + tile, :])
        small = dot_t(lhs[0:rows, 0:depth], low[start : start + tile, :])
        out[:, start : start + tile] = both[:rows] + both[rows:] + small


def kernel(
    bodies, slots, heads, panels,
    neighbours, incident, inverse, blocks, weight,
    out, force,
    stage, inv_high, inv_low, cross_high, cross_low, even, odd, lhs, product, shares,
    load_sem, send_sem, recv_sem, share_send, share_recv,
):
    rows = 2 * heads
    me = lax.axis_index("body")
    depth_z = bodies // 4
    gathered = (even, odd)

    def load(index):
        source = inverse.at[0, index] if index < 2 else blocks.at[0, (index - 2) // 2, (index - 2) % 2]
        return pltpu.make_async_copy(source, stage.at[index], load_sem.at[index])

    for index in range(2 + 2 * slots):
        load(index).start()

    barrier = pltpu.get_barrier_semaphore()
    for bits in range(1, bodies):
        pl.semaphore_signal(barrier, inc=1, device_id={"body": flip(me, bits)})

    def split(index, high, low, column):
        load(index).wait()

        @pl.loop(0, panels // 64)
        def _(step):
            at = pl.ds(pl.multiple_of(step * 64, 64), 64)
            upper, lower = halves(stage[index, at, :])
            high[at, column : column + panels] = upper
            low[at, column : column + panels] = lower

    def send(parity, bits, target, index):
        slot = flip(me, bits)
        return pltpu.make_async_remote_copy(
            src_ref=gathered[parity].at[slot],
            dst_ref=gathered[parity].at[slot],
            send_sem=send_sem.at[index],
            recv_sem=recv_sem.at[parity, slot],
            device_id={"body": flip(me, target)},
        )

    own = [(0, 2), (0, 1)] + [(0, 4 * d) for d in range(1, depth_z)]
    relay = [(2, [1])]
    for d in range(1, depth_z):
        relay.append((4 * d, [2, 1]))
        relay.append((4 * d + 2, [1]))
    every = own + [(slot, target) for slot, targets in relay for target in targets]

    def start_own(parity):
        for index, (slot, target) in enumerate(own):
            send(parity, slot, target, index).start()

    def wait_in(parity, bits):
        slot = flip(me, bits)
        pltpu.make_async_remote_copy(
            src_ref=gathered[parity].at[slot],
            dst_ref=gathered[parity].at[slot],
            send_sem=send_sem.at[0],
            recv_sem=recv_sem.at[parity, slot],
            device_id={"body": flip(me, 1)},
        ).wait_recv()

    def finish_gather(parity):
        index = len(own)
        for slot, targets in relay:
            wait_in(parity, slot)
            for target in targets:
                send(parity, slot, target, index).start()
                index += 1
        for d in range(depth_z):
            wait_in(parity, 4 * d + 1)
            wait_in(parity, 4 * d + 3)

    def wait_sends(parity):
        for index, (slot, target) in enumerate(every):
            send(parity, slot, target, index).wait_send()

    field = incident[0].reshape(rows, panels)
    for part in range(2):
        split(part, inv_high, inv_low, part * panels)
    put_field(lhs, 0, field, heads)
    multiply(lhs, 2 * panels, inv_high, inv_low, product, rows)
    even[me] = product[...]
    pl.semaphore_wait(barrier, bodies - 1)
    start_own(0)
    for part in range(2 * slots):
        split(2 + part, cross_high, cross_low, part * panels)

    def sweep(parity):
        finish_gather(parity)
        for slot in range(slots):
            name = neighbours[0, slot]
            value = gathered[parity][jnp.maximum(name, 0)]
            put_field(lhs, 2 * slot * panels, jnp.where(name >= 0, value, 0.0), heads)
        multiply(lhs, 2 * slots * panels, cross_high, cross_low, product, rows)
        put_field(lhs, 0, incident[0].reshape(rows, panels) - product[...], heads)
        multiply(lhs, 2 * panels, inv_high, inv_low, product, rows)
        wait_sends(parity)

    @pl.loop(0, ITERS // 2)
    def _(pair):
        sweep(0)
        odd[me] = product[...]
        start_own(1)
        sweep(1)

        @pl.when(pair < ITERS // 2 - 1)
        def _():
            even[me] = product[...]
            start_own(0)

    final = product[...]
    out[0] = final.reshape(2, heads, panels)
    scale = jnp.broadcast_to(weight[...], (8, panels))
    sums = [
        lax.dot_general(
            scale, final[c * heads : (c + 1) * heads], (((1,), (1,)), ((), ())),
            precision=lax.Precision.HIGHEST, preferred_element_type=F32,
        )
        for c in range(2)
    ]
    row = lax.broadcasted_iota(jnp.int32, (8, heads), 0)
    shares[me] = jnp.zeros((8, 128), F32)
    shares[me, :, 0:heads] = jnp.where(row == 0, sums[0], sums[1])

    def share(bits):
        return pltpu.make_async_remote_copy(
            src_ref=shares.at[me],
            dst_ref=shares.at[me],
            send_sem=share_send.at[bits],
            recv_sem=share_recv.at[bits],
            device_id={"body": flip(me, bits)},
        )

    def share_in(bits):
        slot = flip(me, bits)
        return pltpu.make_async_remote_copy(
            src_ref=shares.at[slot],
            dst_ref=shares.at[slot],
            send_sem=share_send.at[bits],
            recv_sem=share_recv.at[bits],
            device_id={"body": slot},
        )

    for bits in range(1, bodies):
        share(bits).start()
    for bits in range(1, bodies):
        share_in(bits).wait_recv()
    total = shares[0]
    for other in range(1, bodies):
        total = total + shares[other]
    force[0] = total[0:2, 0:heads]
    for bits in range(1, bodies):
        share(bits).wait_send()


def solution(mesh):
    bodies = mesh.shape["body"]

    def step(incident, self_inverse, cross_blocks, neighbours, panel_weight):
        heads, panels = incident.shape[2:]
        slots = neighbours.shape[1]
        rows = 2 * heads
        vmem = pl.BlockSpec(memory_space=pltpu.VMEM)
        anywhere = pl.BlockSpec(memory_space=pl.ANY)
        copies = 2 * bodies
        return pl.pallas_call(
            functools.partial(kernel, bodies, slots, heads, panels),
            out_shape=(
                jax.ShapeDtypeStruct(incident.shape, F32),
                jax.ShapeDtypeStruct((1, 2, heads), F32),
            ),
            in_specs=[pl.BlockSpec(memory_space=pltpu.SMEM), vmem, anywhere, anywhere, vmem],
            out_specs=(vmem, vmem),
            scratch_shapes=[
                pltpu.VMEM((2 + 2 * slots, panels, panels), F32),
                pltpu.VMEM((panels, 2 * panels), BF16),
                pltpu.VMEM((panels, 2 * panels), BF16),
                pltpu.VMEM((panels, 2 * slots * panels), BF16),
                pltpu.VMEM((panels, 2 * slots * panels), BF16),
                pltpu.VMEM((bodies, rows, panels), F32),
                pltpu.VMEM((bodies, rows, panels), F32),
                pltpu.VMEM((2 * rows, 2 * slots * panels), BF16),
                pltpu.VMEM((rows, panels), F32),
                pltpu.VMEM((bodies, 8, 128), F32),
                pltpu.SemaphoreType.DMA((2 + 2 * slots,)),
                pltpu.SemaphoreType.DMA((copies,)),
                pltpu.SemaphoreType.DMA((2, bodies)),
                pltpu.SemaphoreType.DMA((bodies,)),
                pltpu.SemaphoreType.DMA((bodies,)),
            ],
            compiler_params=pltpu.CompilerParams(
                collective_id=0, has_side_effects=True, vmem_limit_bytes=60 * 1024 * 1024
            ),
        )(neighbours, incident, self_inverse, cross_blocks, panel_weight)

    return jax.shard_map(
        step,
        mesh=mesh,
        in_specs=(
            P(("farm", "body"), None, None, None),
            P(("farm", "body"), None, None, None),
            P(("farm", "body"), None, None, None, None),
            P(("farm", "body"), None),
            P(("farm", "body"), None),
        ),
        out_specs=(P(("farm", "body"), None, None, None), P("farm", None, None)),
        check_vma=False,
    )
```

time: 551 us -> 179 us (0.32); the launches traced: 540 us -> 179 us
  waiting for transfers between devices: 235 us -> 0 us
  matrix products: 224 us -> 0 us
  Pallas kernels: 0 us -> 176 us
  blocking collectives: 32.1 us -> 0 us
  other arithmetic: 20.8 us -> 0 us
  between operations: 15.4 us -> 0.64 us
  local copies, waits for them, and re-layouts: 12.8 us -> 2.78 us
    all_gather x6 -> x0, waiting for transfers between devices: 235 us -> none  [body(): gathered = lax.all_gather(sources[None], 'body', axis=0, tiled=True)]
    dot_general x63 -> x0, matrix products: 224 us -> none  [the longest x31 113 us: complex_apply(): lax.dot_general(stacked, matrix[0], dims, precision=lax.Precision.HIGHEST)]
    pallas_call x0 -> x1, Pallas kernels: none -> 176 us  [step(): pl.pallas_call(functools.partial(kernel, bodies, slots, heads, panels), o...]
    psum x1 -> x0, blocking collectives: 32.1 us -> none  [body(): farm_force = lax.psum(partial_force, 'body')]
    sub x6 -> x0, other arithmetic: 15.2 us -> none  [body(): total - jnp.where(flag_row[slot], complex_apply(blocks[slot], nearby[slot...]
    gather x6 -> x0, local copies, waits for them, and re-layouts: 11.9 us -> none  [body(): nearby = jnp.take(gathered, safe_row, axis=0)]
  transfers between devices with their start and end apart: 6 -> 0, of which waited for: 6 -> 0; matrix products, arithmetic and copies ran while one was open for 0% -> 0% of each run, Pallas kernels for 0% -> 0%
where the time goes in v1:
time: 179 us
  Pallas kernels  176 us (98%)
  local copies, waits for them, and re-layouts  2.78 us (2%)
    pallas_call x1, Pallas kernels, step(): pl.pallas_call(functools.partial(kernel, bodies, slots, heads, panels), o...  176 us

profile of v1, /device:TPU:0, one launch (start us, length us, event | category | flops | bytes accessed | tf_op | source)
XLA Modules:
  0.0 179.3 jit_solution(12447859198302455520)
XLA Ops:
  0.6 175.8 %shard_map.68 = (f32[1,2,16,768]{3,2,1,0:T(8,128)}, f32[1,2,16]{2,1,0:T(2,128)}) custom-call(s32[1,4]{1,0:T(1,128)} %neighbours.1, f32[1,2,16,768]{3,2,1,0:T(8,128)} %incident.1, f32[1,2,768,768]{3,2,1,0:T(8,128)} %inverse.1, f32[1,4,2,768,768]{4,3,2,1,0:T(8,128)} %blocks.1, f32[1,768]{1,0:T(1,128)} %weight.1), custom_call_target="tpu_custom_call" | custom-call | tf_op jit(solution)/shard_map/pallas_call | solution.py:221
  176.5 1.5 copy.9
  178.0 1.2 copy.10

commit v2 on v1

--- a/solution.py
+++ b/solution.py
@@ -8,6 +8,8 @@
 from jax.sharding import PartitionSpec as P
 
 ITERS = 6
+PIECES = 2
+DIRECT = 2
 F32 = jnp.float32
 BF16 = jnp.bfloat16
 
@@ -24,10 +26,6 @@
 def halves(value):
     high = value.astype(BF16)
     return high, (value - high.astype(F32)).astype(BF16)
-
-
-def dot_t(left, right):
-    return lax.dot_general(left, right, (((1,), (1,)), ((), ())), preferred_element_type=F32)
 
 
 def put_field(lhs, column, value, heads):
@@ -45,8 +43,9 @@
     panels = out.shape[1]
     tile = 256
     for start in range(0, panels, tile):
-        both = dot_t(lhs[:, 0:depth], high[start : start + tile, :])
-        small = dot_t(lhs[0:rows, 0:depth], low[start : start + tile, :])
+        at = slice(start, start + tile)
+        both = jnp.dot(lhs[:, 0:depth], high[:, at], preferred_element_type=F32)
+        small = jnp.dot(lhs[0:rows, 0:depth], low[:, at], preferred_element_type=F32)
         out[:, start : start + tile] = both[:rows] + both[rows:] + small
 
 
@@ -73,61 +72,109 @@
     for bits in range(1, bodies):
         pl.semaphore_signal(barrier, inc=1, device_id={"body": flip(me, bits)})
 
-    def split(index, high, low, column):
+    def split(index, high, low, base):
         load(index).wait()
 
-        @pl.loop(0, panels // 64)
+        @pl.loop(0, panels // 128)
         def _(step):
-            at = pl.ds(pl.multiple_of(step * 64, 64), 64)
-            upper, lower = halves(stage[index, at, :])
-            high[at, column : column + panels] = upper
-            low[at, column : column + panels] = lower
-
-    def send(parity, bits, target, index):
-        slot = flip(me, bits)
+            at = pl.ds(pl.multiple_of(step * 128, 128), 128)
+            upper, lower = halves(stage[index, at, :].T)
+            high[base : base + panels, at] = upper
+            low[base : base + panels, at] = lower
+
+    z = me // 4
+
+    def at_z(steps, act):
+        if steps > 0:
+            pl.when(z + steps < depth_z)(act)
+        else:
+            pl.when(z + steps >= 0)(act)
+
+    def send(parity, slot, target, kind, mark, piece):
+        part = pl.ds(piece * (rows // PIECES), rows // PIECES)
         return pltpu.make_async_remote_copy(
-            src_ref=gathered[parity].at[slot],
-            dst_ref=gathered[parity].at[slot],
-            send_sem=send_sem.at[index],
-            recv_sem=recv_sem.at[parity, slot],
-            device_id={"body": flip(me, target)},
+            src_ref=gathered[parity].at[slot, part],
+            dst_ref=gathered[parity].at[slot, part],
+            send_sem=send_sem.at[kind, mark, piece],
+            recv_sem=recv_sem.at[parity, slot, piece],
+            device_id={"body": target},
         )
 
-    own = [(0, 2), (0, 1)] + [(0, 4 * d) for d in range(1, depth_z)]
-    relay = [(2, [1])]
-    for d in range(1, depth_z):
-        relay.append((4 * d, [2, 1]))
-        relay.append((4 * d + 2, [1]))
-    every = own + [(slot, target) for slot, targets in relay for target in targets]
+    def wait_in(parity, slot, piece):
+        send(parity, slot, flip(me, 1), 0, slot, piece).wait_recv()
+
+    def to_core(parity, slot, piece):
+        return send(parity, slot, flip(me, 1), 0, slot, piece)
+
+    def to_row(parity, slot, piece):
+        return send(parity, slot, flip(me, 2), 1, slot, piece)
+
+    def own_sends(parity, act):
+        for steps in range(1, DIRECT + 1):
+            for piece in range(PIECES):
+                for way in (steps, -steps):
+                    target = me + 4 * way
+                    at_z(way, lambda target=target, piece=piece: act(send(parity, me, target, 3, target, piece)))
+                if steps == 1:
+                    act(to_row(parity, me, piece))
+        for piece in range(PIECES):
+            act(to_core(parity, me, piece))
+
+    def column(parity, steps, arrive, act):
+        for piece in range(PIECES):
+            for way in (steps, -steps):
+                def one(way=way, piece=piece):
+                    slot = me + 4 * way
+                    if arrive:
+                        wait_in(parity, slot, piece)
+                    if steps >= DIRECT:
+                        on = -1 if way > 0 else 1
+                        at_z(on, lambda: act(send(parity, slot, me + 4 * on, 2, slot, piece)))
+                    act(to_row(parity, slot, piece))
+                    act(to_core(parity, slot, piece))
+                at_z(way, one)
+
+    def other(parity, steps, arrive, act):
+        for piece in range(PIECES):
+            for way in {steps: None, -steps: None}:
+                def one(way=way, piece=piece):
+                    slot = flip(me, 2) + 4 * way
+                    if arrive:
+                        wait_in(parity, slot, piece)
+                    act(to_core(parity, slot, piece))
+                if way:
+                    at_z(way, one)
+                else:
+                    one()
+
+    def start(copy):
+        copy.start()
+
+    def wait_send(copy):
+        copy.wait_send()
 
     def start_own(parity):
-        for index, (slot, target) in enumerate(own):
-            send(parity, slot, target, index).start()
-
-    def wait_in(parity, bits):
-        slot = flip(me, bits)
-        pltpu.make_async_remote_copy(
-            src_ref=gathered[parity].at[slot],
-            dst_ref=gathered[parity].at[slot],
-            send_sem=send_sem.at[0],
-            recv_sem=recv_sem.at[parity, slot],
-            device_id={"body": flip(me, 1)},
-        ).wait_recv()
+        own_sends(parity, start)
+
+    def relays(parity, arrive, act):
+        for steps in range(depth_z):
+            if steps:
+                column(parity, steps, arrive, act)
+            if steps > 1:
+                other(parity, steps - 2, arrive, act)
+        for steps in range(max(depth_z - 2, 0), depth_z):
+            other(parity, steps, arrive, act)
 
     def finish_gather(parity):
-        index = len(own)
-        for slot, targets in relay:
-            wait_in(parity, slot)
-            for target in targets:
-                send(parity, slot, target, index).start()
-                index += 1
-        for d in range(depth_z):
-            wait_in(parity, 4 * d + 1)
-            wait_in(parity, 4 * d + 3)
+        relays(parity, True, start)
+        for plane in range(depth_z):
+            for row in range(2):
+                for piece in range(PIECES):
+                    wait_in(parity, 4 * plane + 2 * row + 1 - me % 2, piece)
 
     def wait_sends(parity):
-        for index, (slot, target) in enumerate(every):
-            send(parity, slot, target, index).wait_send()
+        own_sends(parity, wait_send)
+        relays(parity, False, wait_send)
 
     field = incident[0].reshape(rows, panels)
     for part in range(2):
@@ -217,7 +264,6 @@
         rows = 2 * heads
         vmem = pl.BlockSpec(memory_space=pltpu.VMEM)
         anywhere = pl.BlockSpec(memory_space=pl.ANY)
-        copies = 2 * bodies
         return pl.pallas_call(
             functools.partial(kernel, bodies, slots, heads, panels),
             out_shape=(
@@ -228,18 +274,18 @@
             out_specs=(vmem, vmem),
             scratch_shapes=[
                 pltpu.VMEM((2 + 2 * slots, panels, panels), F32),
-                pltpu.VMEM((panels, 2 * panels), BF16),
-                pltpu.VMEM((panels, 2 * panels), BF16),
-                pltpu.VMEM((panels, 2 * slots * panels), BF16),
-                pltpu.VMEM((panels, 2 * slots * panels), BF16),
+                pltpu.VMEM((2 * panels, panels), BF16),
+                pltpu.VMEM((2 * panels, panels), BF16),
+                pltpu.VMEM((2 * slots * panels, panels), BF16),
+                pltpu.VMEM((2 * slots * panels, panels), BF16),
                 pltpu.VMEM((bodies, rows, panels), F32),
                 pltpu.VMEM((bodies, rows, panels), F32),
                 pltpu.VMEM((2 * rows, 2 * slots * panels), BF16),
                 pltpu.VMEM((rows, panels), F32),
                 pltpu.VMEM((bodies, 8, 128), F32),
                 pltpu.SemaphoreType.DMA((2 + 2 * slots,)),
-                pltpu.SemaphoreType.DMA((copies,)),
-                pltpu.SemaphoreType.DMA((2, bodies)),
+                pltpu.SemaphoreType.DMA((4, bodies, PIECES)),
+                pltpu.SemaphoreType.DMA((2, bodies, PIECES)),
                 pltpu.SemaphoreType.DMA((bodies,)),
                 pltpu.SemaphoreType.DMA((bodies,)),
             ],

time: 179 us -> 138 us (0.77)
  Pallas kernels: 176 us -> 135 us
    pallas_call x1, Pallas kernels: 176 us -> 135 us  [step(): pl.pallas_call(functools.partial(kernel, bodies, slots, heads, panels), o...]
where the time goes in v2:
time: 138 us
  Pallas kernels  135 us (98%)
  local copies, waits for them, and re-layouts  2.78 us (2%)
    pallas_call x1, Pallas kernels, step(): pl.pallas_call(functools.partial(kernel, bodies, slots, heads, panels), o...  135 us
    unnamed x2, local copies, waits for them, and re-layouts  2.78 us

profile of v2, /device:TPU:0, one launch (start us, length us, event | category | flops | bytes accessed | tf_op | source)
XLA Modules:
  0.0 138.0 jit_solution(17011424557124230121)
XLA Ops:
  0.6 134.6 %shard_map.68 = (f32[1,2,16,768]{3,2,1,0:T(8,128)}, f32[1,2,16]{2,1,0:T(2,128)}) custom-call(s32[1,4]{1,0:T(1,128)} %neighbours.1, f32[1,2,16,768]{3,2,1,0:T(8,128)} %incident.1, f32[1,2,768,768]{3,2,1,0:T(8,128)} %inverse.1, f32[1,4,2,768,768]{4,3,2,1,0:T(8,128)} %blocks.1, f32[1,768]{1,0:T(1,128)} %weight.1), custom_call_target="tpu_custom_call" | custom-call | tf_op jit(solution)/shard_map/pallas_call | solution.py:267
  135.2 1.5 %copy.9 = f32[1,2,16,768]{3,2,1,0:T(8,128)} copy(f32[1,2,16,768]{3,2,1,0:T(8,128)} %get-tuple-element.4) | data formatting | bytes 196608
  136.7 1.2 copy.10

commit v3 on v2

v3 whole, which is shorter than its diff:
```python
import functools

import jax
import jax.numpy as jnp
from jax import lax
from jax.experimental import pallas as pl
from jax.experimental.pallas import tpu as pltpu
from jax.sharding import PartitionSpec as P

ITERS = 6
PIECES = 2
FIRST = 1
DIRECT = 2
F32 = jnp.float32
BF16 = jnp.bfloat16


def flip(index, bits):
    bit = 1
    while bit <= bits:
        if bits & bit:
            index = index + bit - 2 * bit * ((index // bit) % 2)
        bit *= 2
    return index


def pieces(panels):
    first = FIRST * panels // 3
    return [(0, first), (first, panels - first)]


def halves(value):
    high = value.astype(BF16)
    return high, (value - high.astype(F32)).astype(BF16)


def put_field(lhs, column, value, heads):
    rows, width = value.shape
    high, low = halves(value)
    high_t = jnp.concatenate([-high[heads:], high[:heads]], axis=0)
    low_t = jnp.concatenate([-low[heads:], low[:heads]], axis=0)
    lhs[0:rows, column : column + width] = high
    lhs[rows : 2 * rows, column : column + width] = low
    lhs[0:rows, column + width : column + 2 * width] = high_t
    lhs[rows : 2 * rows, column + width : column + 2 * width] = low_t


def multiply(lhs, base, depth, high, low, at, rows):
    deep = slice(base, base + depth)
    both = jnp.dot(lhs[:, 0:depth], high[deep, at], preferred_element_type=F32)
    small = jnp.dot(lhs[0:rows, 0:depth], low[deep, at], preferred_element_type=F32)
    return both[:rows] + both[rows:] + small


def kernel(
    bodies, slots, heads, panels,
    neighbours, incident, inverse, blocks, weight,
    out, force,
    stage, inv_high, inv_low, cross_high, cross_low, lhs, product, shares,
    load_sem, send_sem, recv_sem, share_send, share_recv, *buffers,
):
    rows = 2 * heads
    me = lax.axis_index("body")
    depth_z = bodies // 4
    gathered = (buffers[:PIECES], buffers[PIECES:])
    cuts = [slice(start, start + width) for start, width in pieces(panels)]
    widths = [width for _, width in pieces(panels)]
    tiles = [slice(start, start + 256) for start in range(0, panels, 256)]

    def load(index):
        source = inverse.at[0, index] if index < 2 else blocks.at[0, (index - 2) // 2, (index - 2) % 2]
        return pltpu.make_async_copy(source, stage.at[index], load_sem.at[index])

    for index in range(2 + 2 * slots):
        load(index).start()

    barrier = pltpu.get_barrier_semaphore()
    for bits in range(1, bodies):
        pl.semaphore_signal(barrier, inc=1, device_id={"body": flip(me, bits)})

    def split(index, high, low, part, parts):
        load(index).wait()

        @pl.loop(0, panels // 128)
        def _(step):
            at = pl.ds(pl.multiple_of(step * 128, 128), 128)
            upper, lower = halves(stage[index, at, :].T)
            for piece, cut in enumerate(cuts):
                to = parts * cut.start + part * widths[piece]
                high[to : to + widths[piece], at] = upper[cut]
                low[to : to + widths[piece], at] = lower[cut]

    z = me // 4

    def at_z(steps, act):
        if steps > 0:
            pl.when(z + steps < depth_z)(act)
        else:
            pl.when(z + steps >= 0)(act)

    def send(parity, slot, target, kind, mark, piece):
        return pltpu.make_async_remote_copy(
            src_ref=gathered[parity][piece].at[slot],
            dst_ref=gathered[parity][piece].at[slot],
            send_sem=send_sem.at[kind, mark, piece],
            recv_sem=recv_sem.at[parity, slot, piece],
            device_id={"body": target},
        )

    def wait_in(parity, slot, piece):
        send(parity, slot, flip(me, 1), 0, slot, piece).wait_recv()

    def to_core(parity, slot, piece):
        return send(parity, slot, flip(me, 1), 0, slot, piece)

    def to_row(parity, slot, piece):
        return send(parity, slot, flip(me, 2), 1, slot, piece)

    def own_sends(parity, piece, act):
        for steps in range(1, DIRECT + 1):
            for way in (steps, -steps):
                target = me + 4 * way
                at_z(way, lambda target=target: act(send(parity, me, target, 3, target, piece)))
            if steps == 1:
                act(to_row(parity, me, piece))
        act(to_core(parity, me, piece))

    def column(parity, steps, piece, arrive, act):
        for way in (steps, -steps):
            def one(way=way):
                slot = me + 4 * way
                if arrive:
                    wait_in(parity, slot, piece)
                if steps >= DIRECT:
                    on = -1 if way > 0 else 1
                    at_z(on, lambda: act(send(parity, slot, me + 4 * on, 2, slot, piece)))
                act(to_row(parity, slot, piece))
                act(to_core(parity, slot, piece))
            at_z(way, one)

    def other(parity, steps, piece, arrive, act):
        for way in {steps: None, -steps: None}:
            def one(way=way):
                slot = flip(me, 2) + 4 * way
                if arrive:
                    wait_in(parity, slot, piece)
                act(to_core(parity, slot, piece))
            if way:
                at_z(way, one)
            else:
                one()

    def start(copy):
        copy.start()

    def wait_send(copy):
        copy.wait_send()

    def relay_column(parity, piece):
        for steps in range(1, depth_z):
            column(parity, steps, piece, True, start)
            if steps > 1:
                other(parity, steps - 2, piece, True, start)

    def relay_other(parity, piece):
        for steps in range(max(depth_z - 2, 0), depth_z):
            other(parity, steps, piece, True, start)
        for plane in range(depth_z):
            for row in range(2):
                wait_in(parity, 4 * plane + 2 * row + 1 - me % 2, piece)

    def wait_sends(parity):
        for piece in range(PIECES):
            own_sends(parity, piece, wait_send)
            for steps in range(depth_z):
                if steps:
                    column(parity, steps, piece, False, wait_send)
                other(parity, steps, piece, False, wait_send)

    def solve(parity, value):
        for piece, cut in enumerate(cuts):
            put_field(lhs, 2 * cut.start, value[:, cut], heads)
        for piece, cut in enumerate(cuts):
            part = multiply(lhs, 0, 2 * panels, inv_high, inv_low, cut, rows)
            if parity is None:
                product[:, cut] = part
            else:
                gathered[parity][piece][me] = part
                own_sends(parity, piece, start)

    for part in range(2):
        split(part, inv_high, inv_low, part, 2)
    pl.semaphore_wait(barrier, bodies - 1)
    solve(0, incident[0].reshape(rows, panels))
    for part in range(2 * slots):
        split(2 + part, cross_high, cross_low, part, 2 * slots)

    def sweep(parity):
        for piece in range(PIECES):
            relay_column(parity, piece)
            if piece > 0:
                consume(parity, piece - 1)
        consume(parity, PIECES - 1)
        wait_sends(parity)

    def consume(parity, piece):
        relay_other(parity, piece)
        for slot in range(slots):
            name = neighbours[0, slot]
            value = gathered[parity][piece][jnp.maximum(name, 0)]
            put_field(lhs, 2 * slot * widths[piece], jnp.where(name >= 0, value, 0.0), heads)
        depth = 2 * slots * widths[piece]
        for cut in tiles:
            part = multiply(lhs, 2 * slots * cuts[piece].start, depth, cross_high, cross_low, cut, rows)
            before = incident[0, :, :, cut].reshape(rows, 256) if piece == 0 else product[:, cut]
            product[:, cut] = before - part

    @pl.loop(0, ITERS // 2)
    def _(pair):
        sweep(0)
        solve(1, product[...])
        sweep(1)

        @pl.when(pair < ITERS // 2 - 1)
        def _():
            solve(0, product[...])

    solve(None, product[...])
    final = product[...]
    out[0] = final.reshape(2, heads, panels)
    scale = jnp.broadcast_to(weight[...], (8, panels))
    sums = [
        lax.dot_general(
            scale, final[c * heads : (c + 1) * heads], (((1,), (1,)), ((), ())),
            precision=lax.Precision.HIGHEST, preferred_element_type=F32,
        )
        for c in range(2)
    ]
    row = lax.broadcasted_iota(jnp.int32, (8, heads), 0)
    shares[me] = jnp.zeros((8, 128), F32)
    shares[me, :, 0:heads] = jnp.where(row == 0, sums[0], sums[1])

    def share(bits):
        return pltpu.make_async_remote_copy(
            src_ref=shares.at[me],
            dst_ref=shares.at[me],
            send_sem=share_send.at[bits],
            recv_sem=share_recv.at[bits],
            device_id={"body": flip(me, bits)},
        )

    def share_in(bits):
        slot = flip(me, bits)
        return pltpu.make_async_remote_copy(
            src_ref=shares.at[slot],
            dst_ref=shares.at[slot],
            send_sem=share_send.at[bits],
            recv_sem=share_recv.at[bits],
            device_id={"body": slot},
        )

    for bits in range(1, bodies):
        share(bits).start()
    for bits in range(1, bodies):
        share_in(bits).wait_recv()
    total = shares[0]
    for other in range(1, bodies):
        total = total + shares[other]
    force[0] = total[0:2, 0:heads]
    for bits in range(1, bodies):
        share(bits).wait_send()


def solution(mesh):
    bodies = mesh.shape["body"]

    def step(incident, self_inverse, cross_blocks, neighbours, panel_weight):
        heads, panels = incident.shape[2:]
        slots = neighbours.shape[1]
        rows = 2 * heads
        vmem = pl.BlockSpec(memory_space=pltpu.VMEM)
        anywhere = pl.BlockSpec(memory_space=pl.ANY)
        return pl.pallas_call(
            functools.partial(kernel, bodies, slots, heads, panels),
            out_shape=(
                jax.ShapeDtypeStruct(incident.shape, F32),
                jax.ShapeDtypeStruct((1, 2, heads), F32),
            ),
            in_specs=[pl.BlockSpec(memory_space=pltpu.SMEM), vmem, anywhere, anywhere, vmem],
            out_specs=(vmem, vmem),
            scratch_shapes=[
                pltpu.VMEM((2 + 2 * slots, panels, panels), F32),
                pltpu.VMEM((2 * panels, panels), BF16),
                pltpu.VMEM((2 * panels, panels), BF16),
                pltpu.VMEM((2 * slots * panels, panels), BF16),
                pltpu.VMEM((2 * slots * panels, panels), BF16),
                pltpu.VMEM((2 * rows, 2 * slots * panels), BF16),
                pltpu.VMEM((rows, panels), F32),
                pltpu.VMEM((bodies, 8, 128), F32),
                pltpu.SemaphoreType.DMA((2 + 2 * slots,)),
                pltpu.SemaphoreType.DMA((4, bodies, PIECES)),
                pltpu.SemaphoreType.DMA((2, bodies, PIECES)),
                pltpu.SemaphoreType.DMA((bodies,)),
                pltpu.SemaphoreType.DMA((bodies,)),
                *[pltpu.VMEM((bodies, rows, width), F32) for _, width in pieces(panels)] * 2,
            ],
            compiler_params=pltpu.CompilerParams(
                collective_id=0, has_side_effects=True, vmem_limit_bytes=60 * 1024 * 1024
            ),
        )(neighbours, incident, self_inverse, cross_blocks, panel_weight)

    return jax.shard_map(
        step,
        mesh=mesh,
        in_specs=(
            P(("farm", "body"), None, None, None),
            P(("farm", "body"), None, None, None),
            P(("farm", "body"), None, None, None, None),
            P(("farm", "body"), None),
            P(("farm", "body"), None),
        ),
        out_specs=(P(("farm", "body"), None, None, None), P("farm", None, None)),
        check_vma=False,
    )
```

time: 138 us -> 135 us (0.978)
  Pallas kernels: 135 us -> 131 us
    pallas_call x1, Pallas kernels: 135 us -> 131 us  [step(): pl.pallas_call(functools.partial(kernel, bodies, slots, heads, panels), o...]
where the time goes in v3:
time: 135 us
  Pallas kernels  131 us (97%)
  local copies, waits for them, and re-layouts  2.78 us (2%)
    pallas_call x1, Pallas kernels, step(): pl.pallas_call(functools.partial(kernel, bodies, slots, heads, panels), o...  131 us
    unnamed x2, local copies, waits for them, and re-layouts  2.78 us

profile of v3, /device:TPU:0, one launch (start us, length us, event | category | flops | bytes accessed | tf_op | source)
XLA Modules:
  0.0 134.6 jit_solution(14105578589005701184)
XLA Ops:
  0.6 131.2 %shard_map.68 = (f32[1,2,16,768]{3,2,1,0:T(8,128)}, f32[1,2,16]{2,1,0:T(2,128)}) custom-call(s32[1,4]{1,0:T(1,128)} %neighbours.1, f32[1,2,16,768]{3,2,1,0:T(8,128)} %incident.1, f32[1,2,768,768]{3,2,1,0:T(8,128)} %inverse.1, f32[1,4,2,768,768]{4,3,2,1,0:T(8,128)} %blocks.1, f32[1,768]{1,0:T(1,128)} %weight.1), custom_call_target="tpu_custom_call" | custom-call | tf_op jit(solution)/shard_map/pallas_call | solution.py:283
  131.8 1.5 %copy.9 = f32[1,2,16,768]{3,2,1,0:T(8,128)} copy(f32[1,2,16,768]{3,2,1,0:T(8,128)} %get-tuple-element.4) | data formatting | bytes 196608
  133.4 1.2 copy.10
